TPU v7x, 32 devices: a whole 2x2x4 slice. The times are simulated.
32 devices in a mesh: dp: 4 (over z), ctx: 8 (over y, x, core).
Axes of the slice: x: 2, y: 2, z: 4, core: 2. Of those that a mesh axis runs over, the one named last changes fastest.
Arguments:
- tokens: int32 [4096], P('ctx'), may hold values from 0 to 4
- queries: bfloat16 [4096, 2048], P('ctx', 'dp'), may hold values from -6 to 6
- keys: bfloat16 [4096, 2048], P('ctx', 'dp'), may hold values from -6 to 6
- values: bfloat16 [4096, 2048], P('ctx', 'dp'), may hold values from -6 to 6
- upstream: bfloat16 [4096, 2048], P('ctx', 'dp'), may hold values from -6 to 6
- filter_taps: float32 [4096, 512], P('ctx'), may hold values from -6 to 6
Outputs:
- conv_out: bfloat16 [4096, 2048], P('ctx', 'dp')
- query_grad: bfloat16 [4096, 2048], P('ctx', 'dp')
- key_grad: bfloat16 [4096, 2048], P('ctx', 'dp')
- value_grad: bfloat16 [4096, 2048], P('ctx', 'dp')
- filter_grad: float32 [4096, 512], P('ctx')
Inputs may be any that keep to these rules, and one draw needn't show every extreme that they name: `tokens`: DNA letters: 0 to 3 for A, C, G, T, and 4 for an unknown base, whose positions carry no loss.
All inputs are finite; a program needn't handle non-finite values.
Results may differ from a plain program's by a relative error of at most 0.005.
Values may be sent and summed in bfloat16 or wider, within the bound.
A program may use at most 128 MiB of HBM per device.

v0:
```python
import math

import jax
import jax.numpy as jnp
from jax import lax
from jax.sharding import PartitionSpec as P

two_pi = 2.0 * math.pi


def rotate(count, modulus):
    angle = -two_pi / modulus * (count % modulus).astype(jnp.float32)
    return (jnp.cos(angle), jnp.sin(angle))


def contract(form, table, data):
    return jnp.einsum(form, table, data, precision=lax.Precision.HIGHEST)


def ahead_outer(signal, start, length):
    width = signal.shape[1]
    places = start + jnp.arange(signal.shape[2], dtype=jnp.int32)
    kfreq = jnp.arange(2 * width, dtype=jnp.int32)
    cosine, sine = rotate(kfreq[:, None] * jnp.arange(width, dtype=jnp.int32)[None, :], 2 * width)
    real_part = contract("kp,sprc->skrc", cosine, signal)
    imag_part = contract("kp,sprc->skrc", sine, signal)
    twist_c, twist_s = rotate(kfreq[:, None] * places[None, :], length)
    twist_c = twist_c[None, :, :, None]
    twist_s = twist_s[None, :, :, None]
    return jnp.stack(
        [real_part * twist_c - imag_part * twist_s, real_part * twist_s + imag_part * twist_c]
    )


def ahead_inner(spectrum):
    index = jnp.arange(spectrum.shape[3], dtype=jnp.int32)
    cosine, sine = rotate(index[:, None] * index[None, :], spectrum.shape[3])
    real_part = contract("ji,skic->skjc", cosine, spectrum[0]) - contract(
        "ji,skic->skjc", sine, spectrum[1]
    )
    imag_part = contract("ji,skic->skjc", cosine, spectrum[1]) + contract(
        "ji,skic->skjc", sine, spectrum[0]
    )
    return jnp.stack([real_part, imag_part])


def back_inner(spectrum, kstart, length):
    index = jnp.arange(spectrum.shape[3], dtype=jnp.int32)
    cosine, sine = rotate(index[:, None] * index[None, :], spectrum.shape[3])
    real_part = contract("ji,skjc->skic", cosine, spectrum[0]) + contract(
        "ji,skjc->skic", sine, spectrum[1]
    )
    imag_part = contract("ji,skjc->skic", cosine, spectrum[1]) - contract(
        "ji,skjc->skic", sine, spectrum[0]
    )
    kfreq = kstart + jnp.arange(spectrum.shape[2], dtype=jnp.int32)
    twist_c, twist_s = rotate(kfreq[:, None] * index[None, :], length)
    twist_c = twist_c[None, :, :, None]
    twist_s = twist_s[None, :, :, None]
    return jnp.stack(
        [real_part * twist_c + imag_part * twist_s, imag_part * twist_c - real_part * twist_s]
    )


def back_outer(spectrum, length):
    width = spectrum.shape[2] // 2
    kfreq = jnp.arange(2 * width, dtype=jnp.int32)
    cosine, sine = rotate(kfreq[:, None] * jnp.arange(width, dtype=jnp.int32)[None, :], 2 * width)
    total = contract("kp,skrc->sprc", cosine, spectrum[0]) + contract(
        "kp,skrc->sprc", sine, spectrum[1]
    )
    return total / length


def spectral_terms(spectra):
    u_real, u_imag = (spectra[0, 0], spectra[1, 0])
    z_real, z_imag = (spectra[0, 1], spectra[1, 1])
    filt_r, filt_i = (spectra[0, 2], spectra[1, 2])
    forward_real = filt_r * u_real - filt_i * u_imag
    forward_imag = filt_r * u_imag + filt_i * u_real
    backward_real = filt_r * z_real + filt_i * z_imag
    backward_imag = filt_r * z_imag - filt_i * z_real
    corr_real = u_real * z_real + u_imag * z_imag
    corr_imag = u_real * z_imag - u_imag * z_real
    return jnp.stack(
        [
            jnp.stack([forward_real, backward_real, corr_real]),
            jnp.stack([forward_imag, backward_imag, corr_imag]),
        ]
    )


def on_device(tokens, queries, keys, values, upstream, filter_taps):
    rows = queries.shape[0]
    parts = lax.axis_size("ctx")
    length = 2 * rows * parts
    scale = 1.0 / math.sqrt(rows * parts)
    keep = (tokens != 4).astype(jnp.float32)[:, None]
    grad_in = upstream.astype(jnp.float32) * keep
    query32 = queries.astype(jnp.float32)
    key32 = keys.astype(jnp.float32)
    value32 = values.astype(jnp.float32)
    gated = (key32 * value32).astype(jnp.bfloat16)
    into = (grad_in * query32).astype(jnp.bfloat16)
    paired = jnp.stack([gated, into])
    taps = filter_taps * scale
    sliver = rows // parts
    moved = lax.all_to_all(paired[:, None], "ctx", split_axis=2, concat_axis=1, tiled=True)
    moved_taps = lax.all_to_all(taps[None, None], "ctx", split_axis=2, concat_axis=1, tiled=True)
    signal = jnp.concatenate([moved.astype(jnp.float32), moved_taps], axis=0)
    first = ahead_outer(signal, lax.axis_index("ctx") * sliver, length)
    turned = lax.all_to_all(first, "ctx", split_axis=2, concat_axis=3, tiled=True)
    products = spectral_terms(ahead_inner(turned))
    inner = back_inner(products, 2 * lax.axis_index("ctx"), length)
    spread = lax.all_to_all(inner, "ctx", split_axis=3, concat_axis=2, tiled=True)
    outer = back_outer(spread, length)
    fields = lax.all_to_all(outer, "ctx", split_axis=1, concat_axis=2, tiled=True)[:, 0]
    filter_grad = lax.psum(fields[2], "dp") * scale
    conv = fields[0]
    back = fields[1]
    conv_out = (query32 * conv).astype(jnp.bfloat16)
    query_grad = (grad_in * conv).astype(jnp.bfloat16)
    key_grad = (back * value32).astype(jnp.bfloat16)
    value_grad = (back * key32).astype(jnp.bfloat16)
    return (conv_out, query_grad, key_grad, value_grad, filter_grad)


def solution(mesh):
    placed = (
        P("ctx"),
        P("ctx", "dp"),
        P("ctx", "dp"),
        P("ctx", "dp"),
        P("ctx", "dp"),
        P("ctx", None),
    )
    return jax.shard_map(
        on_device,
        mesh=mesh,
        in_specs=placed,
        out_specs=(P("ctx", "dp"), P("ctx", "dp"), P("ctx", "dp"), P("ctx", "dp"), P("ctx", None)),
        check_vma=False,
    )
```

profile of v0, /device:TPU:0, one launch (start us, length us, event | category | flops | bytes accessed | tf_op | source)
XLA Modules:
  0.0 812.5 jit_solution(15262762479505755769)
XLA Ops:
  7.2 0.8 compare_convert_fusion
  7.9 1.9 fusion.30
  9.8 0.0 copy-done.11
  9.8 0.1 maximum_bitcast_fusion
  9.9 2.0 copy.46
  12.0 5.2 all-to-all-start
  17.2 0.1 multiply_bitcast_fusion.1
  17.3 2.0 copy.48
  19.3 13.3 %all-to-all-done = bf16[2,1,512,512]{3,0,1,2:T(2,128)(2,1)S(1)} async-done(((bf16[2,1,512,512]{3,0,1,2:T(2,128)(2,1)}), bf16[2,1,512,512]{3,0,1,2:T(2,128)(2,1)S(1)}, u32[]{:S(2)}, u32[]{:S(2)}) %all-to-all-start) | async-done | bytes 1048608 | tf_op jit(solution)/shard_map/all_to_all | solution.py:108
  32.6 4.4 all-to-all-start.1
  37.0 0.2 fusion.49
  37.2 0.2 copy.47
  37.4 0.3 convert.1
  37.7 1.2 copy_dynamic-update-slice_fusion
  38.9 13.5 %all-to-all-done.1 = f32[1,1,512,512]{3,1,0,2:T(1,128)} async-done(((f32[1,1,512,512]{3,1,0,2:T(1,128)}), f32[1,1,512,512]{3,1,0,2:T(1,128)}, u32[]{:S(2)}, u32[]{:S(2)}) %all-to-all-start.1) | async-done | bytes 1048608 | tf_op jit(solution)/shard_map/all_to_all | solution.py:109
  52.4 1.3 copy.75
  53.7 0.6 copy_dynamic-update-slice_fusion.1
  54.3 6.1 fusion.58
  60.5 10.2 %fusion.1 = (f32[1,3,16,64,512]{4,2,3,1,0:T(8,128)}, f32[1,3,16,64,512]{4,2,3,1,0:T(8,128)}) fusion(f32[3,64,512,16]{2,3,1,0:T(8,128)S(1)} %fusion.58, f32[16,64]{0,1:T(8,128)S(1)} %get-tuple-element.27, f32[16,64]{0,1:T(8,128)S(1)} %get-tuple-element.26, f32[3,8,64,512]{3,1,2,0:T(8,128)S(1)} %copy_dynamic-update-slice_fusion.1), kind=kOutput, calls=%fused_computation.7 | convolution fusion | flops 160433920 | bytes 22028288 | tf_op jit(solution)/shard_map/kp,sprc->skrc/dot_general | solution.py:17
  70.6 12.1 %pad_maximum_fusion = f32[2,3,16,64,512]{4,2,3,1,0:T(8,128)} fusion(f32[1,3,16,64,512]{4,2,3,1,0:T(8,128)} %get-tuple-element.8, f32[1,3,16,64,512]{4,2,3,1,0:T(8,128)} %get-tuple-element.7), kind=kLoop, calls=%fused_computation | loop fusion | flops 3145728 | bytes 25165824 | tf_op jit(solution)/shard_map/stack | solution.py:30
  82.7 16.4 %copy.51 = f32[2,3,16,64,512]{4,3,1,0,2:T(8,128)} copy(f32[2,3,16,64,512]{4,2,3,1,0:T(8,128)} %pad_maximum_fusion) | data formatting | bytes 25165824 | tf_op jit(solution)/shard_map/stack | solution.py:30
  99.1 5.4 all-to-all-start.2
  104.5 0.0 all-reduce.2.cloned.1.call-start
  104.5 0.2 fusion.67
  104.7 138.8 %all-to-all-done.2 = f32[2,3,16,64,512]{4,3,1,0,2:T(8,128)} async-done(((f32[2,3,16,64,512]{4,3,1,0,2:T(8,128)}), f32[2,3,16,64,512]{4,3,1,0,2:T(8,128)}, u32[]{:S(2)}, u32[]{:S(2)}) %all-to-all-start.2) | async-done | bytes 12582944 | tf_op jit(solution)/shard_map/all_to_all | solution.py:112
  243.5 11.9 %copy.52 = f32[2,3,16,64,512]{4,3,2,1,0:T(8,128)} copy(f32[2,3,16,64,512]{4,3,1,0,2:T(8,128)} %all-to-all-done.2) | data formatting | bytes 25165824 | tf_op jit(solution)/shard_map/all_to_all | solution.py:112
  255.4 9.4 %fusion.127 = (f32[1,3,2,8,64,512]{5,4,2,3,1,0:T(8,128)}, f32[1,3,2,8,64,512]{5,4,2,3,1,0:T(8,128)S(1)}) fusion(f32[2,3,2,8,64,512]{5,4,2,3,1,0:T(8,128)} %bitcast.142), kind=kLoop, calls=%fused_computation.161 | loop fusion | bytes 25165824 | tf_op jit(solution)/shard_map/slice | solution.py:38
  264.8 3.6 copy.53
  268.4 27.0 %fusion.25 = f32[3,2,512,512]{3,2,1,0:T(8,128)} fusion(f32[3,2,512,512]{3,2,1,0:T(8,128)S(1)} %bitcast.138), kind=kOutput, calls=%fused_computation.55 | convolution fusion | flops 9667346432 | bytes 12582912 | tf_op jit(solution)/shard_map/ji,skic->skjc/dot_general | solution.py:17
  295.3 0.8 copy.55
  296.1 27.4 %fusion.23 = f32[3,2,512,512]{3,2,1,0:T(8,128)} fusion(f32[3,2,512,512]{3,2,1,0:T(8,128)S(1)} %bitcast.140), kind=kOutput, calls=%fused_computation.53 | convolution fusion | flops 9667346432 | bytes 12582912 | tf_op jit(solution)/shard_map/ji,skic->skjc/dot_general | solution.py:17
  323.5 25.5 %subtract_bitcast_fusion.1 = f32[1,3,2,512,512]{3,4,2,1,0:T(8,128)S(1)} fusion(f32[3,2,512,512]{3,2,1,0:T(8,128)S(1)} %copy-done, f32[3,2,512,512]{3,2,1,0:T(8,128)S(1)} %bitcast.141), kind=kOutput, calls=%fused_computation.15 | convolution fusion | flops 9668919296 | bytes 18874368 | tf_op jit(solution)/shard_map/ji,skic->skjc/dot_general | solution.py:17
  349.0 30.3 %add_bitcast_fusion.1 = f32[1,3,2,512,512]{3,4,2,1,0:T(8,128)S(1)} fusion(f32[3,2,512,512]{3,2,1,0:T(8,128)} %fusion.23, f32[3,2,512,512]{3,2,1,0:T(8,128)S(1)} %bitcast.139), kind=kOutput, calls=%fused_computation.14 | convolution fusion | flops 9668919296 | bytes 18874368 | tf_op jit(solution)/shard_map/ji,skic->skjc/dot_general | solution.py:17
  379.4 3.6 add_bitcast_fusion.4
  383.0 5.2 subtract_bitcast_fusion.4
  388.2 18.9 %fusion.5 = f32[3,2,512,512]{3,2,1,0:T(8,128)} fusion(f32[1,2,512,512]{2,3,1,0:T(8,128)} %get-tuple-element.14, f32[1,2,512,512]{2,3,1,0:T(8,128)} %get-tuple-element.13, f32[1,2,512,512]{2,3,1,0:T(8,128)} %get-tuple-element.16), kind=kOutput, calls=%fused_computation.17 | convolution fusion | flops 9670492160 | bytes 12582912 | tf_op jit(solution)/shard_map/ji,skjc->skic/dot_general | solution.py:17
  407.1 0.0 copy-done.5
  407.2 16.1 %fusion.4 = f32[3,2,512,512]{3,2,1,0:T(8,128)} fusion(f32[1,2,512,512]{2,3,1,0:T(8,128)S(1)} %copy-done.6, f32[1,2,512,512]{2,3,1,0:T(8,128)S(1)} %copy-done.5, f32[1,2,512,512]{2,3,1,0:T(8,128)S(1)} %copy-done.9), kind=kOutput, calls=%fused_computation.16 | convolution fusion | flops 9670492160 | bytes 12582912 | tf_op jit(solution)/shard_map/ji,skjc->skic/dot_general | solution.py:17
  423.3 15.9 %fusion.6 = f32[3,2,512,512]{3,2,1,0:T(8,128)} fusion(f32[1,2,512,512]{2,3,1,0:T(8,128)S(1)} %copy-done.3, f32[1,2,512,512]{2,3,1,0:T(8,128)S(1)} %copy-done.4, f32[1,2,512,512]{2,3,1,0:T(8,128)S(1)} %copy-done.2), kind=kOutput, calls=%fused_computation.18 | convolution fusion | flops 9670492160 | bytes 12582912 | tf_op jit(solution)/shard_map/ji,skjc->skic/dot_general | solution.py:17
  439.2 27.8 %add_bitcast_fusion = (f32[1,3,2,512,512]{3,4,2,1,0:T(8,128)S(1)}, f32[1,3,2,512,512]{3,4,2,1,0:T(8,128)}) fusion(f32[2,512]{1,0:T(2,128)S(1)} %get-tuple-element.29, f32[2,512]{1,0:T(2,128)S(1)} %get-tuple-element.28, f32[3,2,512,512]{3,2,1,0:T(8,128)} %fusion.4, f32[3,2,512,512]{3,2,1,0:T(8,128)} %fusion.6, f32[3,2,512,512]{3,2,1,0:T(8,128)} %fusion.5, ...), kind=kOutput, calls=%fused_computation.13 | convolution fusion | flops 9683075072 | bytes 37756928 | tf_op jit(solution)/shard_map/ji,skjc->skic/dot_general | solution.py:17
  467.0 8.8 %pad_maximum_fusion.1 = f32[2,3,2,512,512]{3,4,2,1,0:T(8,128)} fusion(f32[1,3,2,512,512]{3,4,2,1,0:T(8,128)} %get-tuple-element.6, f32[1,3,2,512,512]{3,4,2,1,0:T(8,128)S(1)} %get-tuple-element.5), kind=kLoop, calls=%fused_computation.1 | loop fusion | flops 3145728 | bytes 25165824 | tf_op jit(solution)/shard_map/stack | solution.py:60
  475.8 19.1 %copy.59 = f32[2,3,2,512,512]{4,2,1,0,3:T(2,128)} copy(f32[2,3,2,512,512]{3,4,2,1,0:T(8,128)} %pad_maximum_fusion.1) | data formatting | bytes 25165824 | tf_op jit(solution)/shard_map/stack | solution.py:60
  494.9 145.9 %all_to_all.60 = f32[2,3,2,512,512]{4,2,1,0,3:T(2,128)} all-to-all(f32[2,3,2,512,512]{4,2,1,0,3:T(2,128)} %copy.59), channel_id=1, replica_groups=mesh['dp'=4,'ctx'=8] {'ctx'}, dimensions={3} | all-to-all | bytes 25165824 | tf_op jit(solution)/shard_map/all_to_all | solution.py:115
  640.8 12.9 %copy.60 = f32[2,3,2,512,512]{4,3,2,1,0:T(8,128)} copy(f32[2,3,2,512,512]{4,2,1,0,3:T(2,128)} %all_to_all.60) | data formatting | bytes 25165824 | tf_op jit(solution)/shard_map/all_to_all | solution.py:115
  653.7 9.4 %fusion.126 = (f32[1,3,8,2,64,512]{5,4,2,3,1,0:T(8,128)}, f32[1,3,8,2,64,512]{5,4,2,3,1,0:T(8,128)S(1)}) fusion(f32[2,3,8,2,64,512]{5,4,2,3,1,0:T(8,128)} %bitcast.143), kind=kLoop, calls=%fused_computation.160 | loop fusion | bytes 25165824 | tf_op jit(solution)/shard_map/slice | solution.py:70
  663.0 7.4 copy.61
  670.5 8.6 %squeeze.32 = f32[3,16,64,512]{3,1,2,0:T(8,128)} reshape(f32[1,3,8,2,64,512]{5,3,2,4,1,0:T(2,128)} %copy.61) | data formatting | bytes 12582912 | tf_op jit(solution)/shard_map/squeeze | solution.py:69
  679.1 7.1 fusion.56
  686.2 0.0 slice-done.1
  686.2 7.5 copy.62
  693.7 8.6 %squeeze.33 = f32[3,16,64,512]{3,1,2,0:T(8,128)} reshape(f32[1,3,8,2,64,512]{5,3,2,4,1,0:T(2,128)} %copy.62) | data formatting | bytes 12582912 | tf_op jit(solution)/shard_map/squeeze | solution.py:70
  702.3 5.9 multiply_bitcast_fusion
  708.2 1.8 copy.63
  710.1 0.0 copy-start.7
  710.1 0.0 copy-start.8
  710.1 40.4 %all_to_all.61 = f32[3,8,64,512]{3,2,0,1:T(8,128)S(1)} all-to-all(f32[3,8,64,512]{3,2,0,1:T(8,128)S(1)} %copy.63), channel_id=1, replica_groups=mesh['dp'=4,'ctx'=8] {'ctx'}, dimensions={1} | all-to-all | bytes 6291456 | tf_op jit(solution)/shard_map/all_to_all | solution.py:117
  750.5 1.3 fusion.128
  751.8 0.0 all-reduce.2.cloned.1.call-update
  751.8 0.0 copy-done.7
  751.8 0.0 copy-done.8
  751.9 1.2 fusion.10
  753.1 2.5 fusion.16
  755.6 47.6 %all-reduce.2.cloned.1.call-done = f32[512,512]{1,0:T(8,128)} async-done(((f32[512,512]{1,0:T(8,128)}), f32[512,512]{1,0:T(8,128)}) %all-reduce.2.cloned.1.call-update) | async-done | bytes 1048592 | tf_op jit(solution)/shard_map/psum | solution.py:118
  803.2 2.3 broadcast_multiply_fusion
  (26 shorter events, 0.1 us)
Async XLA Ops:
  7.2 10.0 %copy-start.10 = (f32[512,512]{1,0:T(8,128)S(1)}, f32[512,512]{1,0:T(8,128)}, u32[]{:S(2)}) copy-start(f32[512,512]{1,0:T(8,128)} %param.11) | copy-start | bytes 3145732
  7.9 1.9 copy-start.11
  12.0 20.6 %all-to-all-start = ((bf16[2,1,512,512]{3,0,1,2:T(2,128)(2,1)}), bf16[2,1,512,512]{3,0,1,2:T(2,128)(2,1)S(1)}, u32[]{:S(2)}, u32[]{:S(2)}) async-start(bf16[2,1,512,512]{3,0,1,2:T(2,128)(2,1)} %copy.46), calls=%async_computation | async-start | bytes 2097152 | tf_op jit(solution)/shard_map/all_to_all | solution.py:108
  32.6 19.8 %all-to-all-start.1 = ((f32[1,1,512,512]{3,1,0,2:T(1,128)}), f32[1,1,512,512]{3,1,0,2:T(1,128)}, u32[]{:S(2)}, u32[]{:S(2)}) async-start(f32[1,1,512,512]{3,1,0,2:T(1,128)} %copy.48), calls=%async_computation.1 | async-start | bytes 2097152 | tf_op jit(solution)/shard_map/all_to_all | solution.py:109
  99.1 144.4 %all-to-all-start.2 = ((f32[2,3,16,64,512]{4,3,1,0,2:T(8,128)}), f32[2,3,16,64,512]{4,3,1,0,2:T(8,128)}, u32[]{:S(2)}, u32[]{:S(2)}) async-start(f32[2,3,16,64,512]{4,3,1,0,2:T(8,128)} %copy.51), calls=%async_computation.2 | async-start | bytes 25165824 | tf_op jit(solution)/shard_map/all_to_all | solution.py:112
  104.5 698.7 %all-reduce.2.cloned.1.call-start = ((), (), s32[]{:S(2)}) async-start(), calls=%async_computation.5 | async-start | bytes 2097152 | tf_op jit(solution)/shard_map/psum | solution.py:118
  296.1 27.4 %copy-start = (f32[3,2,512,512]{3,2,1,0:T(8,128)S(1)}, f32[3,2,512,512]{3,2,1,0:T(8,128)}, u32[]{:S(2)}) copy-start(f32[3,2,512,512]{3,2,1,0:T(8,128)} %fusion.25) | copy-start | bytes 18874372
  388.2 18.9 %copy-start.5 = (f32[1,2,512,512]{2,3,1,0:T(8,128)S(1)}, f32[1,2,512,512]{2,3,1,0:T(8,128)}, u32[]{:S(2)}) copy-start(f32[1,2,512,512]{2,3,1,0:T(8,128)} %get-tuple-element.13) | copy-start | bytes 6291460
  388.2 18.9 %copy-start.6 = (f32[1,2,512,512]{2,3,1,0:T(8,128)S(1)}, f32[1,2,512,512]{2,3,1,0:T(8,128)}, u32[]{:S(2)}) copy-start(f32[1,2,512,512]{2,3,1,0:T(8,128)} %get-tuple-element.14) | copy-start | bytes 6291460
  388.2 18.9 %copy-start.9 = (f32[1,2,512,512]{2,3,1,0:T(8,128)S(1)}, f32[1,2,512,512]{2,3,1,0:T(8,128)}, u32[]{:S(2)}) copy-start(f32[1,2,512,512]{2,3,1,0:T(8,128)} %get-tuple-element.16) | copy-start | bytes 6291460
  407.1 16.1 %copy-start.2 = (f32[1,2,512,512]{2,3,1,0:T(8,128)S(1)}, f32[1,2,512,512]{2,3,1,0:T(8,128)}, u32[]{:S(2)}) copy-start(f32[1,2,512,512]{2,3,1,0:T(8,128)} %get-tuple-element.11) | copy-start | bytes 6291460
  407.2 16.1 %copy-start.3 = (f32[1,2,512,512]{2,3,1,0:T(8,128)S(1)}, f32[1,2,512,512]{2,3,1,0:T(8,128)}, u32[]{:S(2)}) copy-start(f32[1,2,512,512]{2,3,1,0:T(8,128)} %get-tuple-element.12) | copy-start | bytes 6291460
  407.2 16.1 %copy-start.4 = (f32[1,2,512,512]{2,3,1,0:T(8,128)S(1)}, f32[1,2,512,512]{2,3,1,0:T(8,128)}, u32[]{:S(2)}) copy-start(f32[1,2,512,512]{2,3,1,0:T(8,128)} %get-tuple-element.15) | copy-start | bytes 6291460
  670.5 15.7 %slice-start = ((s8[6291456]{0:T(1024)(128)(4,1)}), s8[2097152]{0:T(1024)(128)(4,1)S(1)}, s32[]{:S(2)}) async-start(s8[6291456]{0:T(1024)(128)(4,1)} %bitcast.144), calls=%async_computation.6 | async-start | bytes 4194304
  679.1 7.1 slice-start.1
  693.7 8.6 %copy-start.1 = (f32[3,64,512,8]{2,3,1,0:T(8,128)S(1)}, f32[3,64,512,8]{2,3,1,0:T(8,128)}, u32[]{:S(2)}) copy-start(f32[3,64,512,8]{2,3,1,0:T(8,128)} %fusion.56) | copy-start | bytes 9437188
  710.1 41.8 %copy-start.7 = (bf16[512,512]{1,0:T(8,128)(2,1)S(1)}, bf16[512,512]{1,0:T(8,128)(2,1)}, u32[]{:S(2)}) copy-start(bf16[512,512]{1,0:T(8,128)(2,1)} %param.9) | copy-start | bytes 1572868
  710.1 41.8 %copy-start.8 = (bf16[512,512]{1,0:T(8,128)(2,1)S(1)}, bf16[512,512]{1,0:T(8,128)(2,1)}, u32[]{:S(2)}) copy-start(bf16[512,512]{1,0:T(8,128)(2,1)} %param.8) | copy-start | bytes 1572868
  750.5 2.5 copy-start.12
Sparse Core Ops, SparseCore 0:
  752.0 51.1 all-reduce.1
where the time goes:
time: 817 us; the launch traced here: 813 us
  matrix products  218 us (27%)
  waiting for transfers between devices  213 us (26%)
  blocking collectives  186 us (23%)
  local copies, waits for them, and re-layouts  126 us (15%)
  other arithmetic  39.3 us (5%)
  starting transfers between devices  15 us (2%)
  between operations  14.5 us (2%)
    dot_general x12, matrix products, contract(): return jnp.einsum(form, table, data, precision=lax.Precision.HIGHEST)  218 us
    all_to_all x1, blocking collectives, on_device(): lax.all_to_all(inner, 'ctx', split_axis=3, concat_axis=2, tiled=True)  146 us
    all_to_all x1, waiting for transfers between devices, on_device(): lax.all_to_all(first, 'ctx', split_axis=2, concat_axis=3, tiled=True)  139 us
    psum x1, waiting for transfers between devices, on_device(): filter_grad = lax.psum(fields[2], 'dp') * scale  47.6 us
    all_to_all x1, blocking collectives, on_device(): lax.all_to_all(outer, 'ctx', split_axis=1, concat_axis=2, tiled=True)[:, 0]  40.4 us
    another operation x1, local copies, waits for them, and re-layouts, back_inner(): jnp.stack([real_part * twist_c + imag_part * twist_s, imag_part * twist_c...  19.1 us
    slice x2, local copies, waits for them, and re-layouts, back_outer(): spectrum[1]  16.8 us
    another operation x1, local copies, waits for them, and re-layouts, ahead_outer(): jnp.stack([real_part * twist_c - imag_part * twist_s, real_part * twist_s...  16.4 us
  transfers between devices with their start and end apart: 4, of which 4 were waited for; matrix products, arithmetic and copies ran while one was open for 1% of the time, Pallas kernels for 0%

commit v1 on v0

--- a/solution.py
+++ b/solution.py
@@ -2,10 +2,15 @@
 
 import jax
 import jax.numpy as jnp
+import ml_dtypes
+import numpy as np
 from jax import lax
+from jax.experimental import pallas as pl
+from jax.experimental.pallas import tpu as pltpu
 from jax.sharding import PartitionSpec as P
 
 two_pi = 2.0 * math.pi
+TILE = 16
 
 
 def rotate(count, modulus):
@@ -125,6 +130,180 @@
     return (conv_out, query_grad, key_grad, value_grad, filter_grad)
 
 
+def split(table):
+    high = table.astype(ml_dtypes.bfloat16)
+    low = (table - high.astype(np.float64)).astype(ml_dtypes.bfloat16)
+    return (high, low)
+
+
+def tables():
+    p = np.arange(32)
+    rows = [np.ones(32), np.cos(np.pi * p)]
+    weight = [1.0, 1.0]
+    for k in range(1, 32):
+        rows.append(np.cos(2 * np.pi * k * p / 64))
+        rows.append(-np.sin(2 * np.pi * k * p / 64))
+        weight += [2.0, 2.0]
+    lead = np.stack(rows)
+    eye = np.eye(TILE)
+    ahead = np.concatenate(split(np.kron(lead, eye)), axis=1)
+    behind = lead.T * np.array(weight)[None, :] / 8192.0
+    behind = np.concatenate(split(np.kron(behind, eye)), axis=1)
+    angle = 2 * np.pi * np.outer(np.arange(128), np.arange(128)) / 128
+    cosine, sine = np.cos(angle), np.sin(angle)
+    inner = np.block([[cosine, sine], [-sine, cosine]])
+    inner_ahead = np.stack(split(inner))
+    inner_behind = np.stack(split(inner.T))
+    twist = 2 * np.pi * np.outer(np.arange(33), np.arange(128)) / 8192
+    twist = np.stack([np.cos(twist), -np.sin(twist)], axis=1).astype(np.float32)
+    twist = np.ascontiguousarray(np.broadcast_to(twist[..., None], (33, 2, 128, 128)))
+    return (ahead, behind, inner_ahead, inner_behind, twist)
+
+
+def dot(left, right):
+    return jnp.dot(left, right, preferred_element_type=jnp.float32)
+
+
+def dot_split(table_ref, data):
+    high = data.astype(jnp.bfloat16)
+    low = (data - high.astype(jnp.float32)).astype(jnp.bfloat16)
+    return dot(table_ref[0], high) + dot(table_ref[0], low) + dot(table_ref[1], high)
+
+
+def transform(z_ref, h_ref, tabs, a_ref, s_ref, emit):
+    ahead, behind, inner_ahead, inner_behind, twist = tabs
+    chunk = 8
+
+    def first(step, _):
+        places = pl.ds(pl.multiple_of(step * TILE, TILE), TILE)
+        data = jnp.concatenate(
+            [z_ref[:, places, :].reshape(32 * TILE, 128), h_ref[:, places, :].reshape(32 * TILE, 128)],
+            axis=1,
+        )
+        for part in range(64 // chunk):
+            lines = slice(part * chunk * TILE, (part + 1) * chunk * TILE)
+            out = dot(ahead[lines, : 32 * TILE], data) + dot(ahead[lines, 32 * TILE :], data)
+            a_ref[part * chunk : (part + 1) * chunk, places, :] = out.reshape(chunk, TILE, 256)
+        return 0
+
+    lax.fori_loop(0, 128 // TILE, first, 0)
+
+    lane = lax.broadcasted_iota(jnp.int32, (128, 128), 1)
+    sign = jnp.where(lane < 64, 1.0, -1.0)
+
+    def middle(k, real_part, imag_part):
+        cosine, sine = twist[k, 0], twist[k, 1]
+        halves = []
+        for side in (0, 128):
+            re = real_part[:, side : side + 128]
+            if imag_part is None:
+                halves.append((re * cosine, re * sine))
+            else:
+                im = imag_part[:, side : side + 128]
+                halves.append((re * cosine - im * sine, re * sine + im * cosine))
+        data = jnp.concatenate(
+            [jnp.concatenate([halves[0][0], halves[1][0]], axis=1),
+             jnp.concatenate([halves[0][1], halves[1][1]], axis=1)], axis=0)
+        spec = dot_split(inner_ahead, data)
+        ur, ui = spec[:128, :128], spec[128:, :128]
+        hr, hi = spec[:128, 128:], spec[128:, 128:] * sign
+        zr, zi = pltpu.roll(ur, 64, 1), pltpu.roll(ui, 64, 1)
+        real_part = jnp.concatenate([hr * ur - hi * ui, ur * zr + ui * zi], axis=1)
+        imag_part = jnp.concatenate([hr * ui + hi * ur, ur * zi - ui * zr], axis=1)
+        time = dot_split(inner_behind, jnp.concatenate([real_part, imag_part], axis=0))
+        outs = []
+        for side in (0, 128):
+            re, im = time[:128, side : side + 128], time[128:, side : side + 128]
+            outs.append((re * cosine + im * sine, im * cosine - re * sine))
+        return (
+            jnp.concatenate([outs[0][0], outs[1][0]], axis=1).astype(jnp.bfloat16),
+            jnp.concatenate([outs[0][1], outs[1][1]], axis=1).astype(jnp.bfloat16),
+        )
+
+    s_ref[0] = middle(0, a_ref[0], None)[0]
+    s_ref[1] = middle(32, a_ref[1], None)[0]
+
+    def second(k, _):
+        real_part, imag_part = middle(k, a_ref[2 * k], a_ref[2 * k + 1])
+        s_ref[2 * k] = real_part
+        s_ref[2 * k + 1] = imag_part
+        return 0
+
+    lax.fori_loop(1, 32, second, 0)
+
+    def last(step, _):
+        places = pl.ds(pl.multiple_of(step * TILE, TILE), TILE)
+        data = s_ref[:, places, :].reshape(64 * TILE, 256)
+        for part in range(32 // chunk):
+            lines = slice(part * chunk * TILE, (part + 1) * chunk * TILE)
+            out = dot(behind[lines, : 64 * TILE], data) + dot(behind[lines, 64 * TILE :], data)
+            emit(part * chunk, chunk, places, out.reshape(chunk, TILE, 256))
+        return 0
+
+    lax.fori_loop(0, 128 // TILE, last, 0)
+
+
+def local_kernel(z_ref, h_ref, *refs):
+    tabs, (pair_ref, corr_ref, a_ref, s_ref) = refs[:5], refs[5:]
+
+    def emit(start, count, places, out):
+        pair_ref[start : start + count, places, :] = out[:, :, :128].astype(jnp.bfloat16)
+        corr_ref[start : start + count, places, :] = out[:, :, 128:].astype(jnp.bfloat16)
+
+    transform(z_ref, h_ref, tabs, a_ref, s_ref, emit)
+
+
+def local_convolution(paired, taps):
+    tabs = [jnp.asarray(t) for t in tables()]
+    whole = pl.BlockSpec(memory_space=pltpu.VMEM)
+    shape = jax.ShapeDtypeStruct((32, 128, 128), jnp.bfloat16)
+    return pl.pallas_call(
+        local_kernel,
+        out_shape=(shape, shape),
+        in_specs=[whole] * 7,
+        out_specs=(whole, whole),
+        scratch_shapes=[pltpu.VMEM((64, 128, 256), jnp.float32), pltpu.VMEM((64, 128, 256), jnp.bfloat16)],
+        compiler_params=pltpu.CompilerParams(vmem_limit_bytes=48 * 1024 * 1024),
+    )(paired, taps, *tabs)
+
+
+def by_channel(tokens, queries, keys, values, upstream, filter_taps):
+    rows = queries.shape[0]
+    scale = 1.0 / 64.0
+    keep = (tokens != 4).astype(jnp.float32)[:, None]
+    grad_in = upstream.astype(jnp.float32) * keep
+    query32 = queries.astype(jnp.float32)
+    key32 = keys.astype(jnp.float32)
+    value32 = values.astype(jnp.float32)
+    gated = (key32 * value32).astype(jnp.bfloat16)
+    into = (grad_in * query32).astype(jnp.bfloat16)
+    taps = (filter_taps * scale).astype(jnp.bfloat16)
+    cut = lambda array: array.reshape(rows, 8, 64).transpose(1, 0, 2)
+    paired = jnp.concatenate([cut(gated), cut(into)], axis=2)
+    taps = cut(taps)
+    paired = lax.all_to_all(paired, "ctx", split_axis=0, concat_axis=0, tiled=True)
+    taps = lax.all_to_all(taps, "ctx", split_axis=0, concat_axis=0, tiled=True)
+    taps = jnp.concatenate([taps, taps], axis=2)
+    pair, corr = local_convolution(paired.reshape(32, 128, 128), taps.reshape(32, 128, 128))
+    pair = lax.all_to_all(pair.reshape(8, rows, 128), "ctx", split_axis=0, concat_axis=0, tiled=True)
+    corr = corr.reshape(8, rows, 128)[:, :, :64]
+    corr = lax.all_to_all(corr, "ctx", split_axis=0, concat_axis=0, tiled=True)
+    join = lambda array: array.transpose(1, 0, 2).reshape(rows, 512).astype(jnp.float32)
+    conv, back = join(pair[:, :, :64]), join(pair[:, :, 64:])
+    filter_grad = lax.psum(join(corr), "dp") * scale
+    conv_out = (query32 * conv).astype(jnp.bfloat16)
+    query_grad = (grad_in * conv).astype(jnp.bfloat16)
+    key_grad = (back * value32).astype(jnp.bfloat16)
+    value_grad = (back * key32).astype(jnp.bfloat16)
+    return (conv_out, query_grad, key_grad, value_grad, filter_grad)
+
+
+def either(*args):
+    parts = lax.axis_size("ctx")
+    fits = parts == 8 and args[1].shape == (512, 512) and args[5].shape == (512, 512)
+    return by_channel(*args) if fits else on_device(*args)
+
+
 def solution(mesh):
     placed = (
         P("ctx"),
@@ -135,7 +314,7 @@
         P("ctx", None),
     )
     return jax.shard_map(
-        on_device,
+        either,
         mesh=mesh,
         in_specs=placed,
         out_specs=(P("ctx", "dp"), P("ctx", "dp"), P("ctx", "dp"), P("ctx", "dp"), P("ctx", None)),

time: 817 us -> 173 us (0.21)
  matrix products: 218 us -> 0 us
  blocking collectives: 186 us -> 0 us
  waiting for transfers between devices: 213 us -> 73.9 us
  local copies, waits for them, and re-layouts: 126 us -> 18.9 us
  Pallas kernels: 0 us -> 40.7 us
  other arithmetic: 39.3 us -> 8.83 us
    dot_general x12 -> x0, matrix products: 218 us -> none  [contract(): return jnp.einsum(form, table, data, precision=lax.Precision.HIGHEST)]
    all_to_all x2 -> x0, blocking collectives: 186 us -> none  [the longest x1 146 us: on_device(): lax.all_to_all(inner, 'ctx', split_axis=3, concat_axis=2, tiled=True)]
    all_to_all x3 -> x4, waiting for transfers between devices: 166 us -> 40.5 us  [the longest x1 13.3 us: by_channel(): lax.all_to_all(paired, 'ctx', split_axis=0, concat_axis=0, tiled=True)]
    pallas_call x0 -> x1, Pallas kernels: none -> 40.7 us  [local_convolution(): pl.pallas_call(local_kernel, out_shape=(shape, shape), in_specs=[whole] *...]
    slice x7 -> x0, local copies, waits for them, and re-layouts: 39.3 us -> none  [the longest x2 16.8 us: back_outer(): spectrum[1]]
    another operation x2 -> x0, local copies, waits for them, and re-layouts: 35.5 us -> none  [the longest x1 19.1 us: back_inner(): jnp.stack([real_part * twist_c + imag_part * twist_s, imag_part * twist_c...]
    all_to_all x3 -> x1, local copies, waits for them, and re-layouts: 25 us -> 0.65 us  [by_channel(): lax.all_to_all(paired, 'ctx', split_axis=0, concat_axis=0, tiled=True)]
    another operation x3 -> x0, other arithmetic: 22.8 us -> none  [the longest x1 12.1 us: ahead_outer(): jnp.stack([real_part * twist_c - imag_part * twist_s, real_part * twist_s...]
  transfers between devices with their start and end apart: 4 -> 5, of which waited for: 4 -> 5; matrix products, arithmetic and copies ran while one was open for 1% -> 10% of each run, Pallas kernels for 0% -> 0%
where the time goes in v1:
time: 173 us; the launch traced here: 172 us
  waiting for transfers between devices  73.9 us (43%)
  Pallas kernels  40.7 us (24%)
  local copies, waits for them, and re-layouts  18.9 us (11%)
  starting transfers between devices  15.8 us (9%)
  between operations  14.3 us (8%)
  other arithmetic  8.83 us (5%)
    pallas_call x1, Pallas kernels, local_convolution(): pl.pallas_call(local_kernel, out_shape=(shape, shape), in_specs=[whole] *...  40.7 us
    psum x1, waiting for transfers between devices, by_channel(): filter_grad = lax.psum(join(corr), 'dp') * scale  33.4 us
    unnamed x51, local copies, waits for them, and re-layouts  16.3 us
    all_to_all x1, waiting for transfers between devices, by_channel(): lax.all_to_all(paired, 'ctx', split_axis=0, concat_axis=0, tiled=True)  13.3 us
    all_to_all x1, waiting for transfers between devices, by_channel(): lax.all_to_all(pair.reshape(8, rows, 128), 'ctx', split_axis=0, concat_ax...  13.1 us
    all_to_all x1, waiting for transfers between devices, by_channel(): corr = lax.all_to_all(corr, 'ctx', split_axis=0, concat_axis=0, tiled=True)  8.34 us
    all_to_all x1, waiting for transfers between devices, by_channel(): taps = lax.all_to_all(taps, 'ctx', split_axis=0, concat_axis=0, tiled=True)  5.74 us
    all_to_all x1, starting transfers between devices, by_channel(): taps = lax.all_to_all(taps, 'ctx', split_axis=0, concat_axis=0, tiled=True)  5.17 us
  transfers between devices with their start and end apart: 5, of which 5 were waited for; matrix products, arithmetic and copies ran while one was open for 10% of the time, Pallas kernels for 0%

profile of v1, /device:TPU:0, one launch (start us, length us, event | category | flops | bytes accessed | tf_op | source)
XLA Modules:
  0.0 172.4 jit_solution(13750801303708790120)
XLA Ops:
  7.2 0.0 copy-start.16
  7.2 1.6 copy.27
  8.8 0.0 copy-start.17
  8.8 0.9 multiply_convert_fusion
  9.7 5.2 %all-to-all-start.1 = ((bf16[8,512,64]{1,2,0:T(8,128)(2,1)}), bf16[8,512,64]{1,2,0:T(8,128)(2,1)S(1)}, u32[]{:S(2)}, u32[]{:S(2)}) async-start(bf16[8,512,64]{1,2,0:T(8,128)(2,1)} %bitcast.6), calls=%async_computation.1 | async-start | bytes 1048576 | tf_op jit(solution)/shard_map/all_to_all | solution.py:285
  14.9 0.0 copy-done.16
  14.9 0.0 copy-start.19
  14.9 0.0 copy-start.18
  14.9 0.2 copy.23
  15.1 0.0 copy-done.17
  15.1 0.0 copy-start.4
  15.2 0.2 copy.24
  15.4 0.0 copy-start.6
  15.4 0.1 fusion.3
  15.5 0.1 copy-done.19
  15.6 0.4 copy-done.18
  16.0 0.2 copy.22
  16.2 0.0 copy-start.8
  16.2 1.4 copy.25
  17.6 0.0 copy-done.4
  17.6 0.0 copy-start.10
  17.7 0.2 fusion
  17.8 0.0 copy-done.6
  17.8 1.1 pad_maximum_fusion
  18.9 0.0 copy-done.8
  18.9 5.7 %all-to-all-done.1 = bf16[8,512,64]{1,2,0:T(8,128)(2,1)S(1)} async-done(((bf16[8,512,64]{1,2,0:T(8,128)(2,1)}), bf16[8,512,64]{1,2,0:T(8,128)(2,1)S(1)}, u32[]{:S(2)}, u32[]{:S(2)}) %all-to-all-start.1) | async-done | bytes 524320 | tf_op jit(solution)/shard_map/all_to_all | solution.py:285
  24.6 0.8 copy-done.12
  25.4 0.0 copy-done.10
  25.4 3.6 %all-to-all-start = ((bf16[8,512,128]{1,2,0:T(8,128)(2,1)}), bf16[8,512,128]{1,2,0:T(8,128)(2,1)S(1)}, u32[]{:S(2)}, u32[]{:S(2)}) async-start(bf16[8,512,128]{1,2,0:T(8,128)(2,1)} %pad_maximum_fusion), calls=%async_computation | async-start | bytes 2097152 | tf_op jit(solution)/shard_map/all_to_all | solution.py:284
  29.0 1.4 pad_maximum_fusion.1
  30.4 0.0 copy-start.2
  30.4 0.7 copy.28
  31.0 13.3 %all-to-all-done = bf16[8,512,128]{1,2,0:T(8,128)(2,1)S(1)} async-done(((bf16[8,512,128]{1,2,0:T(8,128)(2,1)}), bf16[8,512,128]{1,2,0:T(8,128)(2,1)S(1)}, u32[]{:S(2)}, u32[]{:S(2)}) %all-to-all-start) | async-done | bytes 1048608 | tf_op jit(solution)/shard_map/all_to_all | solution.py:284
  44.3 0.7 copy.26
  45.0 0.0 copy-done.2
  45.0 0.0 copy-start.3
  45.0 0.9 copy-done.3
  46.0 40.7 %shard_map.146 = (bf16[32,128,128]{2,1,0:T(8,128)(2,1)S(1)}, bf16[32,128,128]{2,1,0:T(8,128)(2,1)S(1)}) custom-call(bf16[32,128,128]{2,1,0:T(8,128)(2,1)S(1)} %bitcast.30, bf16[32,128,128]{2,1,0:T(8,128)(2,1)S(1)} %bitcast.29, bf16[1024,1024]{1,0:T(8,128)(2,1)} %constant.14.clone.refs_0_, bf16[512,2048]{1,0:T(8,128)(2,1)} %constant.15.clone.refs_1_, ...), custom_call_target="tpu_custom_call" | custom-call | tf_op jit(solution)/shard_map/pallas_call | solution.py:260
  86.6 0.0 copy-start
  86.6 1.0 copy-done
  87.6 1.1 copy.36
  88.7 3.5 %all-to-all-start.3 = ((bf16[8,512,64]{1,2,0:T(8,128)(2,1)}), bf16[8,512,64]{1,2,0:T(8,128)(2,1)S(1)}, u32[]{:S(2)}, u32[]{:S(2)}) async-start(bf16[8,512,64]{1,2,0:T(8,128)(2,1)} %copy.36), calls=%async_computation.3 | async-start | bytes 1048576 | tf_op jit(solution)/shard_map/all_to_all | solution.py:290
  92.2 0.0 copy-done.1
  92.2 1.3 copy.29
  93.6 8.3 %all-to-all-done.3 = bf16[8,512,64]{1,2,0:T(8,128)(2,1)S(1)} async-done(((bf16[8,512,64]{1,2,0:T(8,128)(2,1)}), bf16[8,512,64]{1,2,0:T(8,128)(2,1)S(1)}, u32[]{:S(2)}, u32[]{:S(2)}) %all-to-all-start.3) | async-done | bytes 524320 | tf_op jit(solution)/shard_map/all_to_all | solution.py:290
  101.9 0.8 copy-done.13
  102.7 3.6 %all-to-all-start.2 = ((bf16[8,512,128]{1,2,0:T(8,128)(2,1)}), bf16[8,512,128]{1,2,0:T(8,128)(2,1)S(1)}, u32[]{:S(2)}, u32[]{:S(2)}) async-start(bf16[8,512,128]{1,2,0:T(8,128)(2,1)} %copy.29), calls=%async_computation.2 | async-start | bytes 2097152 | tf_op jit(solution)/shard_map/all_to_all | solution.py:288
  106.3 0.0 all-reduce.2.cloned.1.call-start
  106.3 2.1 %convert_element_type.89 = f32[8,512,64]{1,2,0:T(8,128)} convert(bf16[8,512,64]{1,2,0:T(8,128)(2,1)} %copy-done.13) | non-fusion elementwise | flops 262144 | bytes 1572864 | tf_op jit(solution)/shard_map/convert_element_type | solution.py:291
  108.5 0.0 all-reduce.2.cloned.1.call-update
  108.5 13.1 %all-to-all-done.2 = bf16[8,512,128]{1,2,0:T(8,128)(2,1)S(1)} async-done(((bf16[8,512,128]{1,2,0:T(8,128)(2,1)}), bf16[8,512,128]{1,2,0:T(8,128)(2,1)S(1)}, u32[]{:S(2)}, u32[]{:S(2)}) %all-to-all-start.2) | async-done | bytes 1048608 | tf_op jit(solution)/shard_map/all_to_all | solution.py:288
  121.6 0.0 copy-done.5
  121.6 0.0 copy-done.7
  121.6 0.0 copy-done.9
  121.6 0.0 copy-done.11
  121.6 1.7 %fusion.2 = (bf16[512,512]{0,1:T(8,128)(2,1)}, bf16[512,512]{0,1:T(8,128)(2,1)}, bf16[512,512]{0,1:T(8,128)(2,1)}, bf16[512,512]{0,1:T(8,128)(2,1)}) fusion(bf16[512,512]{0,1:T(8,128)(2,1)S(1)} %copy-done.5, bf16[8,512,128]{1,2,0:T(8,128)(2,1)S(1)} %all-to-all-done.2, f32[512]{0:T(512)S(1)} %compare_convert_fusion, bf16[512,512]{0,1:T(8,128)(2,1)S(1)} %copy-done.11, ...), kind=kLoop, calls=%fused_computation.7 | loop fusion | flops 3932160 | bytes 5244928 | tf_op jit(solution)/shard_map/convert_element_type | solution.py:297
  123.4 2.1 %copy.34 = bf16[512,512]{1,0:T(8,128)(2,1)} copy(bf16[512,512]{0,1:T(8,128)(2,1)} %get-tuple-element.14) | data formatting | bytes 1048576
  125.5 2.1 %copy.32 = bf16[512,512]{1,0:T(8,128)(2,1)} copy(bf16[512,512]{0,1:T(8,128)(2,1)} %get-tuple-element.15) | data formatting | bytes 1048576
  127.6 0.0 copy-done.15
  127.6 1.0 copy.33
  128.6 1.0 copy.31
  129.6 33.4 %all-reduce.2.cloned.1.call-done = f32[512,512]{0,1:T(8,128)} async-done(((f32[512,512]{0,1:T(8,128)}), f32[512,512]{0,1:T(8,128)}) %all-reduce.2.cloned.1.call-update) | async-done | bytes 1048592 | tf_op jit(solution)/shard_map/psum | solution.py:293
  163.0 1.3 broadcast_multiply_fusion
  164.3 1.3 copy.35
  (11 shorter events, 0.0 us)
Async XLA Ops:
  7.2 7.7 %copy-start.16 = (bf16[512,512]{1,0:T(8,128)(2,1)S(1)}, bf16[512,512]{1,0:T(8,128)(2,1)}, u32[]{:S(2)}) copy-start(bf16[512,512]{1,0:T(8,128)(2,1)} %param.13) | copy-start | bytes 1572868
  8.8 6.3 %copy-start.17 = (bf16[512,512]{1,0:T(8,128)(2,1)S(1)}, bf16[512,512]{1,0:T(8,128)(2,1)}, u32[]{:S(2)}) copy-start(bf16[512,512]{1,0:T(8,128)(2,1)} %param.14) | copy-start | bytes 1572868
  9.7 14.9 %all-to-all-start.1 = ((bf16[8,512,64]{1,2,0:T(8,128)(2,1)}), bf16[8,512,64]{1,2,0:T(8,128)(2,1)S(1)}, u32[]{:S(2)}, u32[]{:S(2)}) async-start(bf16[8,512,64]{1,2,0:T(8,128)(2,1)} %bitcast.6), calls=%async_computation.1 | async-start | bytes 1048576 | tf_op jit(solution)/shard_map/all_to_all | solution.py:285
  14.9 0.7 copy-start.19
  14.9 1.0 copy-start.18
  15.1 2.5 %copy-start.4 = (bf16[512,512]{0,1:T(8,128)(2,1)}, bf16[512,512]{0,1:T(8,128)(2,1)S(1)}, u32[]{:S(2)}) copy-start(bf16[512,512]{0,1:T(8,128)(2,1)S(1)} %copy.23) | copy-start | bytes 1572868
  15.4 2.4 %copy-start.6 = (bf16[512,512]{0,1:T(8,128)(2,1)}, bf16[512,512]{0,1:T(8,128)(2,1)S(1)}, u32[]{:S(2)}) copy-start(bf16[512,512]{0,1:T(8,128)(2,1)S(1)} %copy.24) | copy-start | bytes 1572868
  16.2 2.7 %copy-start.8 = (bf16[512,512]{0,1:T(8,128)(2,1)}, bf16[512,512]{0,1:T(8,128)(2,1)S(1)}, u32[]{:S(2)}) copy-start(bf16[512,512]{0,1:T(8,128)(2,1)S(1)} %copy.22) | copy-start | bytes 1572868
  17.6 7.8 %copy-start.10 = (bf16[512,512]{0,1:T(8,128)(2,1)}, bf16[512,512]{0,1:T(8,128)(2,1)S(1)}, u32[]{:S(2)}) copy-start(bf16[512,512]{0,1:T(8,128)(2,1)S(1)} %copy.25) | copy-start | bytes 1572868
  24.6 0.8 copy-start.12
  25.4 18.9 %all-to-all-start = ((bf16[8,512,128]{1,2,0:T(8,128)(2,1)}), bf16[8,512,128]{1,2,0:T(8,128)(2,1)S(1)}, u32[]{:S(2)}, u32[]{:S(2)}) async-start(bf16[8,512,128]{1,2,0:T(8,128)(2,1)} %pad_maximum_fusion), calls=%async_computation | async-start | bytes 2097152 | tf_op jit(solution)/shard_map/all_to_all | solution.py:284
  30.4 14.6 %copy-start.2 = (bf16[2,256,256]{2,1,0:T(8,128)(2,1)S(1)}, bf16[2,256,256]{2,1,0:T(8,128)(2,1)}, u32[]{:S(2)}) copy-start(bf16[2,256,256]{2,1,0:T(8,128)(2,1)} %constant.17.clone.refs_3_) | copy-start | bytes 786436
  45.0 1.0 copy-start.3
  86.6 1.0 copy-start
  87.6 4.6 %copy-start.1 = (bf16[32,128,128]{2,1,0:T(8,128)(2,1)S(1)}, bf16[32,128,128]{2,1,0:T(8,128)(2,1)}, u32[]{:S(2)}) copy-start(bf16[32,128,128]{2,1,0:T(8,128)(2,1)} %copy-done) | copy-start | bytes 3145732
  88.7 13.2 %all-to-all-start.3 = ((bf16[8,512,64]{1,2,0:T(8,128)(2,1)}), bf16[8,512,64]{1,2,0:T(8,128)(2,1)S(1)}, u32[]{:S(2)}, u32[]{:S(2)}) async-start(bf16[8,512,64]{1,2,0:T(8,128)(2,1)} %copy.36), calls=%async_computation.3 | async-start | bytes 1048576 | tf_op jit(solution)/shard_map/all_to_all | solution.py:290
  93.6 28.1 %copy-start.5 = (bf16[512,512]{0,1:T(8,128)(2,1)S(1)}, bf16[512,512]{0,1:T(8,128)(2,1)}, u32[]{:S(2)}) copy-start(bf16[512,512]{0,1:T(8,128)(2,1)} %copy-done.4) | copy-start | bytes 1572868
  93.6 28.1 %copy-start.7 = (bf16[512,512]{0,1:T(8,128)(2,1)S(1)}, bf16[512,512]{0,1:T(8,128)(2,1)}, u32[]{:S(2)}) copy-start(bf16[512,512]{0,1:T(8,128)(2,1)} %copy-done.6) | copy-start | bytes 1572868
  93.6 28.1 %copy-start.9 = (bf16[512,512]{0,1:T(8,128)(2,1)S(1)}, bf16[512,512]{0,1:T(8,128)(2,1)}, u32[]{:S(2)}) copy-start(bf16[512,512]{0,1:T(8,128)(2,1)} %copy-done.8) | copy-start | bytes 1572868
  93.6 28.1 %copy-start.11 = (bf16[512,512]{0,1:T(8,128)(2,1)S(1)}, bf16[512,512]{0,1:T(8,128)(2,1)}, u32[]{:S(2)}) copy-start(bf16[512,512]{0,1:T(8,128)(2,1)} %copy-done.10) | copy-start | bytes 1572868
  101.9 0.8 copy-start.13
  102.7 18.9 %all-to-all-start.2 = ((bf16[8,512,128]{1,2,0:T(8,128)(2,1)}), bf16[8,512,128]{1,2,0:T(8,128)(2,1)S(1)}, u32[]{:S(2)}, u32[]{:S(2)}) async-start(bf16[8,512,128]{1,2,0:T(8,128)(2,1)} %copy.29), calls=%async_computation.2 | async-start | bytes 2097152 | tf_op jit(solution)/shard_map/all_to_all | solution.py:288
  106.3 56.7 %all-reduce.2.cloned.1.call-start = ((), (), s32[]{:S(2)}) async-start(), calls=%async_computation.4 | async-start | bytes 2097152 | tf_op jit(solution)/shard_map/psum | solution.py:293
  123.4 4.2 %copy-start.15 = (bf16[512,512]{0,1:T(8,128)(2,1)S(1)}, bf16[512,512]{0,1:T(8,128)(2,1)}, u32[]{:S(2)}) copy-start(bf16[512,512]{0,1:T(8,128)(2,1)} %get-tuple-element.16) | copy-start | bytes 1572868
  123.4 5.2 %copy-start.14 = (bf16[512,512]{0,1:T(8,128)(2,1)S(1)}, bf16[512,512]{0,1:T(8,128)(2,1)}, u32[]{:S(2)}) copy-start(bf16[512,512]{0,1:T(8,128)(2,1)} %get-tuple-element.17) | copy-start | bytes 1572868
Sparse Core Ops, SparseCore 0:
  109.5 53.4 all-reduce.1

commit v2 on v1

--- a/solution.py
+++ b/solution.py
@@ -11,6 +11,7 @@
 
 two_pi = 2.0 * math.pi
 TILE = 16
+MESH = pl.DeviceIdType.MESH
 
 
 def rotate(count, modulus):
@@ -170,7 +171,7 @@
     return dot(table_ref[0], high) + dot(table_ref[0], low) + dot(table_ref[1], high)
 
 
-def transform(z_ref, h_ref, tabs, a_ref, s_ref, emit):
+def transform(z_ref, h_ref, tabs, a_ref, s_ref):
     ahead, behind, inner_ahead, inner_behind, twist = tabs
     chunk = 8
 
@@ -229,73 +230,187 @@
         s_ref[2 * k + 1] = imag_part
         return 0
 
-    lax.fori_loop(1, 32, second, 0)
-
-    def last(step, _):
+    lax.fori_loop(1, 32, second, 0, unroll=2)
+
+
+def low_half(shape):
+    return lax.broadcasted_iota(jnp.int32, shape, len(shape) - 1) < 64
+
+
+def swap(array):
+    return pltpu.roll(array, 64, array.ndim - 1)
+
+
+def block(ref, index):
+    return ref.at[pl.ds(4 * index, 4)]
+
+
+def whole_kernel(
+    keep_ref, q_ref, k_ref, v_ref, up_ref, taps_ref,
+    ahead, behind, inner_ahead, inner_behind, twist,
+    conv_out, query_grad, key_grad, value_grad, filter_grad,
+    zs, z_ref, ts, tr, h_ref, a_ref, s_ref, ps, pr, cs, cr, ct, fr, fg,
+    z_sems, t_sems, p_sems, c_sems, f_sems, g_sems,
+):
+    me = lax.axis_index("ctx")
+    row = lax.axis_index("dp")
+    f32, bf16 = jnp.float32, jnp.bfloat16
+
+    barrier = pltpu.get_barrier_semaphore()
+    for step in range(1, 8):
+        pl.semaphore_signal(barrier, 1, device_id={"ctx": lax.rem(me + step, 8)}, device_id_type=MESH)
+    for step in range(1, 4):
+        pl.semaphore_signal(barrier, 1, device_id={"dp": lax.rem(row + step, 4)}, device_id_type=MESH)
+
+    low = low_half((512, 128))
+    for pair in range(4):
+        cols = slice(128 * pair, 128 * pair + 128)
+        gated = k_ref[:, cols].astype(f32) * v_ref[:, cols].astype(f32)
+        into = up_ref[:, cols].astype(f32) * keep_ref[...] * q_ref[:, cols].astype(f32)
+        zs[8 * pair : 8 * pair + 4] = jnp.where(low, gated, swap(into)).astype(bf16).reshape(4, 128, 128)
+        zs[8 * pair + 4 : 8 * pair + 8] = jnp.where(low, swap(gated), into).astype(bf16).reshape(4, 128, 128)
+        taps = taps_ref[:, cols] * (1.0 / 64.0)
+        top, bottom = taps[:256], taps[256:]
+        ts[2 * pair] = jnp.where(low[:256], top, swap(bottom)).astype(bf16)
+        ts[2 * pair + 1] = jnp.where(low[:256], swap(top), bottom).astype(bf16)
+
+    pl.semaphore_wait(barrier, 10)
+
+    def to_ctx(source, target, sems, step, peer):
+        return pltpu.make_async_remote_copy(
+            source, target, sems.at[0, step], sems.at[1, step],
+            device_id={"ctx": peer}, device_id_type=MESH)
+
+    def to_dp(source, target, sems, step):
+        return pltpu.make_async_remote_copy(
+            source, target, sems.at[0, step], sems.at[1, step],
+            device_id={"dp": lax.rem(row + step, 4)}, device_id_type=MESH)
+
+    moves = []
+    for step in range(1, 8):
+        peer = lax.rem(me + step, 8)
+        moves.append(to_ctx(block(zs, peer), block(z_ref, me), z_sems, step, peer))
+        moves.append(to_ctx(ts.at[peer], tr.at[me], t_sems, step, peer))
+    for move in moves:
+        move.start()
+    z_ref[pl.ds(4 * me, 4)] = zs[pl.ds(4 * me, 4)]
+    tr[me] = ts[me]
+    for move in moves:
+        move.wait()
+
+    def unpack(source, _):
+        packed = tr[source].astype(f32)
+        turned = swap(packed)
+        half = low_half((256, 128))
+        h_ref[pl.ds(4 * source, 2)] = jnp.where(half, packed, turned).astype(bf16).reshape(2, 128, 128)
+        h_ref[pl.ds(4 * source + 2, 2)] = jnp.where(half, turned, packed).astype(bf16).reshape(2, 128, 128)
+        return 0
+
+    lax.fori_loop(0, 8, unpack, 0)
+    transform(z_ref, h_ref, (ahead, behind, inner_ahead, inner_behind, twist), a_ref, s_ref)
+
+    def correlate(step, _):
         places = pl.ds(pl.multiple_of(step * TILE, TILE), TILE)
-        data = s_ref[:, places, :].reshape(64 * TILE, 256)
-        for part in range(32 // chunk):
-            lines = slice(part * chunk * TILE, (part + 1) * chunk * TILE)
+        data = s_ref[:, places, 128:].reshape(64 * TILE, 128)
+        half = low_half((4, TILE, 128))
+        for part in range(4):
+            out = dot(behind[128 * part : 128 * part + 128, : 64 * TILE], data).reshape(8, TILE, 128)
+            cs[:, part, places, :] = jnp.where(half, out[:4], swap(out[4:])).astype(bf16)
+        return 0
+
+    lax.fori_loop(0, 128 // TILE, correlate, 0)
+    summed = [to_dp(cs.at[lax.rem(row + step, 4)], cr.at[step], c_sems, step) for step in range(1, 4)]
+    for move in summed:
+        move.start()
+
+    returned = []
+    for turn in range(1, 5):
+        part = lax.rem(me // 2 + turn, 4)
+
+        def convolve(step, _):
+            places = pl.ds(pl.multiple_of(step * TILE, TILE), TILE)
+            data = s_ref[:, places, :128].reshape(64 * TILE, 128)
+            lines = pl.ds(pl.multiple_of(128 * part, 128), 128)
             out = dot(behind[lines, : 64 * TILE], data) + dot(behind[lines, 64 * TILE :], data)
-            emit(part * chunk, chunk, places, out.reshape(chunk, TILE, 256))
-        return 0
-
-    lax.fori_loop(0, 128 // TILE, last, 0)
-
-
-def local_kernel(z_ref, h_ref, *refs):
-    tabs, (pair_ref, corr_ref, a_ref, s_ref) = refs[:5], refs[5:]
-
-    def emit(start, count, places, out):
-        pair_ref[start : start + count, places, :] = out[:, :, :128].astype(jnp.bfloat16)
-        corr_ref[start : start + count, places, :] = out[:, :, 128:].astype(jnp.bfloat16)
-
-    transform(z_ref, h_ref, tabs, a_ref, s_ref, emit)
-
-
-def local_convolution(paired, taps):
+            ps[pl.ds(8 * part, 8), places, :] = out.reshape(8, TILE, 128).astype(bf16)
+            return 0
+
+        lax.fori_loop(0, 128 // TILE, convolve, 0)
+        peers = [lax.rem(me + 2 * turn, 8), (me // 2 + turn) % 4 * 2 + 1 - me % 2]
+        for side, peer in enumerate(peers):
+            if turn == 4 and side == 0:
+                continue
+            move = to_ctx(block(ps, peer), block(pr, me), p_sems, 2 * turn - 2 + side, peer)
+            move.start()
+            returned.append(move)
+    pr[pl.ds(4 * me, 4)] = ps[pl.ds(4 * me, 4)]
+
+    for move in summed:
+        move.wait()
+    total = cs[row].astype(f32)
+    for step in range(1, 4):
+        total = total + cr[step].astype(f32)
+    ct[...] = total.astype(bf16)
+    spread = []
+    for step in range(1, 8):
+        peer = lax.rem(me + step, 8)
+        move = to_ctx(ct.at[peer // 2], fr.at[me], f_sems, step, peer)
+        move.start()
+        spread.append(move)
+    fr[me] = ct[me // 2]
+    for move in spread:
+        move.wait()
+    odd = lax.rem(me, 2)
+    half = low_half((128, 128))
+    for pair in range(4):
+        first, second = fr[2 * pair].astype(f32), fr[2 * pair + 1].astype(f32)
+        even_case = jnp.where(half, first, swap(second))
+        odd_case = jnp.where(half, swap(first), second)
+        fg[row, :, 128 * pair : 128 * pair + 128] = jnp.where(odd == 0, even_case, odd_case).astype(bf16)
+    gathered = [to_dp(fg.at[row], fg.at[row], g_sems, step) for step in range(1, 4)]
+    for move in gathered:
+        move.start()
+
+    for move in returned:
+        move.wait()
+    for pair in range(4):
+        cols = slice(128 * pair, 128 * pair + 128)
+        first = pr[8 * pair : 8 * pair + 4].reshape(512, 128).astype(f32)
+        second = pr[8 * pair + 4 : 8 * pair + 8].reshape(512, 128).astype(f32)
+        conv = jnp.where(low, first, swap(second))
+        back = jnp.where(low, swap(first), second)
+        conv_out[:, cols] = (q_ref[:, cols].astype(f32) * conv).astype(bf16)
+        query_grad[:, cols] = (up_ref[:, cols].astype(f32) * keep_ref[...] * conv).astype(bf16)
+        key_grad[:, cols] = (back * v_ref[:, cols].astype(f32)).astype(bf16)
+        value_grad[:, cols] = (back * k_ref[:, cols].astype(f32)).astype(bf16)
+    for move in gathered:
+        move.wait()
+    for quarter in range(4):
+        filter_grad[128 * quarter : 128 * quarter + 128, :] = fg[quarter].astype(f32) * (1.0 / 64.0)
+
+
+def by_channel(tokens, queries, keys, values, upstream, filter_taps):
+    keep = jnp.broadcast_to((tokens != 4).astype(jnp.float32)[:, None], (512, 128))
     tabs = [jnp.asarray(t) for t in tables()]
-    whole = pl.BlockSpec(memory_space=pltpu.VMEM)
-    shape = jax.ShapeDtypeStruct((32, 128, 128), jnp.bfloat16)
+    vmem = pl.BlockSpec(memory_space=pltpu.VMEM)
+    bf16, f32 = jnp.bfloat16, jnp.float32
+    wide = jax.ShapeDtypeStruct((512, 512), bf16)
+    full, packed = pltpu.VMEM((32, 128, 128), bf16), pltpu.VMEM((8, 256, 128), bf16)
+    quarter = pltpu.VMEM((4, 4, 128, 128), bf16)
     return pl.pallas_call(
-        local_kernel,
-        out_shape=(shape, shape),
-        in_specs=[whole] * 7,
-        out_specs=(whole, whole),
-        scratch_shapes=[pltpu.VMEM((64, 128, 256), jnp.float32), pltpu.VMEM((64, 128, 256), jnp.bfloat16)],
-        compiler_params=pltpu.CompilerParams(vmem_limit_bytes=48 * 1024 * 1024),
-    )(paired, taps, *tabs)
-
-
-def by_channel(tokens, queries, keys, values, upstream, filter_taps):
-    rows = queries.shape[0]
-    scale = 1.0 / 64.0
-    keep = (tokens != 4).astype(jnp.float32)[:, None]
-    grad_in = upstream.astype(jnp.float32) * keep
-    query32 = queries.astype(jnp.float32)
-    key32 = keys.astype(jnp.float32)
-    value32 = values.astype(jnp.float32)
-    gated = (key32 * value32).astype(jnp.bfloat16)
-    into = (grad_in * query32).astype(jnp.bfloat16)
-    taps = (filter_taps * scale).astype(jnp.bfloat16)
-    cut = lambda array: array.reshape(rows, 8, 64).transpose(1, 0, 2)
-    paired = jnp.concatenate([cut(gated), cut(into)], axis=2)
-    taps = cut(taps)
-    paired = lax.all_to_all(paired, "ctx", split_axis=0, concat_axis=0, tiled=True)
-    taps = lax.all_to_all(taps, "ctx", split_axis=0, concat_axis=0, tiled=True)
-    taps = jnp.concatenate([taps, taps], axis=2)
-    pair, corr = local_convolution(paired.reshape(32, 128, 128), taps.reshape(32, 128, 128))
-    pair = lax.all_to_all(pair.reshape(8, rows, 128), "ctx", split_axis=0, concat_axis=0, tiled=True)
-    corr = corr.reshape(8, rows, 128)[:, :, :64]
-    corr = lax.all_to_all(corr, "ctx", split_axis=0, concat_axis=0, tiled=True)
-    join = lambda array: array.transpose(1, 0, 2).reshape(rows, 512).astype(jnp.float32)
-    conv, back = join(pair[:, :, :64]), join(pair[:, :, 64:])
-    filter_grad = lax.psum(join(corr), "dp") * scale
-    conv_out = (query32 * conv).astype(jnp.bfloat16)
-    query_grad = (grad_in * conv).astype(jnp.bfloat16)
-    key_grad = (back * value32).astype(jnp.bfloat16)
-    value_grad = (back * key32).astype(jnp.bfloat16)
-    return (conv_out, query_grad, key_grad, value_grad, filter_grad)
+        whole_kernel,
+        out_shape=(wide, wide, wide, wide, jax.ShapeDtypeStruct((512, 512), f32)),
+        in_specs=[vmem] * 11,
+        out_specs=(vmem,) * 5,
+        scratch_shapes=[
+            full, full, packed, packed, full,
+            pltpu.VMEM((64, 128, 256), f32), pltpu.VMEM((64, 128, 256), bf16),
+            full, full, quarter, quarter,
+            pltpu.VMEM((4, 128, 128), bf16), pltpu.VMEM((8, 128, 128), bf16), pltpu.VMEM((4, 128, 512), bf16),
+        ] + [pltpu.SemaphoreType.DMA((2, 8))] * 6,
+        compiler_params=pltpu.CompilerParams(
+            collective_id=0, has_side_effects=True, vmem_limit_bytes=56 * 1024 * 1024),
+    )(keep, queries, keys, values, upstream, filter_taps, *tabs)
 
 
 def either(*args):

time: 173 us -> 97.1 us (0.56)
  waiting for transfers between devices: 73.9 us -> 0 us
  Pallas kernels: 40.7 us -> 86.7 us
  starting transfers between devices: 15.8 us -> 0 us
  between operations: 14.3 us -> 0.67 us
  local copies, waits for them, and re-layouts: 18.9 us -> 7.29 us
  other arithmetic: 8.83 us -> 0.68 us
    pallas_call x1, Pallas kernels: 40.7 us -> 86.7 us  [by_channel(): pl.pallas_call(whole_kernel, out_shape=(wide, wide, wide, wide, jax.Shape...]
    all_to_all x4 -> x0, waiting for transfers between devices: 40.5 us -> none  [the longest x1 13.3 us: by_channel(): lax.all_to_all(paired, 'ctx', split_axis=0, concat_axis=0, tiled=True)]
    psum x1 -> x0, waiting for transfers between devices: 33.4 us -> none  [by_channel(): filter_grad = lax.psum(join(corr), 'dp') * scale]
    all_to_all x4 -> x0, starting transfers between devices: 15.8 us -> none  [the longest x1 5.17 us: by_channel(): taps = lax.all_to_all(taps, 'ctx', split_axis=0, concat_axis=0, tiled=True)]
    unnamed x51 -> x11, local copies, waits for them, and re-layouts: 16.3 us -> 6.45 us
    convert_element_type x6 -> x1, other arithmetic: 5.1 us -> 0.68 us  [by_channel(): (tokens != 4).astype(jnp.float32)[:, None]]
    concatenate x2 -> x0, other arithmetic: 2.42 us -> none  [the longest x1 1.36 us: by_channel(): taps = jnp.concatenate([taps, taps], axis=2)]
  transfers between devices with their start and end apart: 5 -> 0, of which waited for: 5 -> 0; matrix products, arithmetic and copies ran while one was open for 10% -> 0% of each run, Pallas kernels for 0% -> 0%
where the time goes in v2:
time: 97.1 us; the launch traced here: 95.3 us
  Pallas kernels  86.7 us (89%)
  local copies, waits for them, and re-layouts  7.29 us (8%)
    pallas_call x1, Pallas kernels, by_channel(): pl.pallas_call(whole_kernel, out_shape=(wide, wide, wide, wide, jax.Shape...  86.7 us
    unnamed x11, local copies, waits for them, and re-layouts  6.45 us

profile of v2, /device:TPU:0, one launch (start us, length us, event | category | flops | bytes accessed | tf_op | source)
XLA Modules:
  0.0 95.3 jit_solution(6873325424943403486)
XLA Ops:
  0.6 0.7 compare_convert_fusion
  1.3 0.8 broadcast_in_dim.2.keep_ref
  2.2 86.7 %shard_map.146 = (bf16[512,512]{1,0:T(8,128)(2,1)}, bf16[512,512]{1,0:T(8,128)(2,1)}, bf16[512,512]{1,0:T(8,128)(2,1)}, bf16[512,512]{1,0:T(8,128)(2,1)}, f32[512,512]{1,0:T(8,128)}) custom-call(f32[512,128]{1,0:T(8,128)} %broadcast_in_dim.2.keep_ref, bf16[512,512]{1,0:T(8,128)(2,1)} %q_ref.1, bf16[512,512]{1,0:T(8,128)(2,1)} %k_ref.1, ...), custom_call_target="tpu_custom_call" | custom-call | tf_op jit(solution)/shard_map/pallas_call | solution.py:400
  88.8 0.0 copy-start.2
  88.8 0.0 copy-start.1
  88.9 0.0 copy-start
  88.9 2.0 %copy.21 = bf16[512,512]{1,0:T(8,128)(2,1)} copy(bf16[512,512]{1,0:T(8,128)(2,1)} %get-tuple-element.10) | data formatting | bytes 1048576
  90.9 1.9 %copy.22 = bf16[512,512]{1,0:T(8,128)(2,1)} copy(bf16[512,512]{1,0:T(8,128)(2,1)} %get-tuple-element.11) | data formatting | bytes 1048576
  92.7 0.0 copy-done.2
  92.8 0.8 copy.23
  93.5 0.0 copy-done.1
  93.5 0.8 copy.24
  94.3 0.0 copy-done
  94.3 1.0 %copy.25 = f32[512,512]{1,0:T(8,128)} copy(f32[512,512]{1,0:T(8,128)S(1)} %copy-done) | data formatting | bytes 2097152
Async XLA Ops:
  88.8 3.9 %copy-start.2 = (bf16[512,512]{1,0:T(8,128)(2,1)S(1)}, bf16[512,512]{1,0:T(8,128)(2,1)}, u32[]{:S(2)}) copy-start(bf16[512,512]{1,0:T(8,128)(2,1)} %get-tuple-element.12) | copy-start | bytes 1572868
  88.8 4.7 %copy-start.1 = (bf16[512,512]{1,0:T(8,128)(2,1)S(1)}, bf16[512,512]{1,0:T(8,128)(2,1)}, u32[]{:S(2)}) copy-start(bf16[512,512]{1,0:T(8,128)(2,1)} %get-tuple-element.13) | copy-start | bytes 1572868
  88.9 5.5 %copy-start = (f32[512,512]{1,0:T(8,128)S(1)}, f32[512,512]{1,0:T(8,128)}, u32[]{:S(2)}) copy-start(f32[512,512]{1,0:T(8,128)} %get-tuple-element.14) | copy-start | bytes 3145732
